TPU v7x, 512 devices: a whole 4x8x8 slice. The times are simulated.
512 devices in a mesh: nodes: 64 (over z, x, core), hid: 8 (over y).
Axes of the slice: x: 4, y: 8, z: 8, core: 2. Of those that a mesh axis runs over, the one named last changes fastest.
Arguments:
- latents: bfloat16 [16384, 512], P('nodes'), may hold values from -16 to 16
- cotangent: bfloat16 [16384, 512], P('nodes'), may hold values from -16 to 16
- w_send: bfloat16 [512, 2048], P(None, 'hid'), may hold values from -0.1875 to 0.1875
- w_recv: bfloat16 [512, 2048], P(None, 'hid'), may hold values from -0.1875 to 0.1875
- bias: float32 [2048], P('hid'), may hold values from -1 to 1
- w_out: bfloat16 [2048, 512], P('hid'), may hold values from -0.125 to 0.125
- fine_sender: int32 [98304], P('nodes'), may hold values from 0 to 383
- fine_receiver: int32 [98304], P('nodes'), may hold values from 0 to 255
- fine_valid: int32 [98304], P('nodes'), may hold values from 0 to 1, as said below
- send_rows: int32 [64, 64, 4], P('nodes'), may hold values from 0 to 7
- coarse_slot: int32 [32768], P('nodes'), may hold values from 0 to 255
- coarse_receiver: int32 [32768], P('nodes'), may hold values from 0 to 255
- coarse_valid: int32 [32768], P('nodes'), may hold values from 0 to 1, as said below
Outputs:
- grad_nodes: float32 [16384, 512], P('nodes', 'hid')
- grad_send: float32 [512, 2048], P('nodes', 'hid')
- grad_recv: float32 [512, 2048], P('nodes', 'hid')
- grad_out: float32 [2048, 512], P('hid', 'nodes')
- grad_bias: float32 [2048], P(('hid', 'nodes'))
Inputs may be any that keep to these rules, and one draw needn't show every extreme that they name: `fine_sender`: index into the receiving block's nodes extended by 64 nodes of the previous block in front and 64 of the next block behind. `fine_valid`: 1 marks a live edge, 0 a padding slot. `send_rows`: a node among the first 8 of block b. `coarse_slot`: slot q names the row that block q // 4 sends to the edge's block in its slot q % 4. `coarse_valid`: 1 marks a live edge, 0 a padding slot.
All inputs are finite; a program needn't handle non-finite values.
Results may differ from a plain program's by a relative error of at most 0.0065.
Values may be sent and summed in bfloat16 or wider, within the bound.
A program may use at most 64 MiB of HBM per device.

v0:
```python
import jax
import jax.numpy as jnp
from jax import lax
from jax.sharding import PartitionSpec as P

COARSE_NODES = 8
COARSE_CAP = 4
HALO = 64


def extended_2(block, sides, width):
    for axis, dim in sides:
        count = lax.axis_size(axis)
        forward = [(i, i + 1) for i in range(count - 1)]
        backward = [(target, source) for source, target in forward]
        low = lax.ppermute(
            lax.slice_in_dim(block, block.shape[dim] - width, None, axis=dim), axis, forward
        )
        high = lax.ppermute(lax.slice_in_dim(block, 0, width, axis=dim), axis, backward)
        block = jnp.concatenate([low, block, high], axis=dim)
    return block


def one_hot_rows(count, index, dtype):
    return (jnp.arange(count, dtype=jnp.int32)[:, None] == index[None, :]).astype(dtype)


def split_right(left, right):
    upper = right.astype(jnp.bfloat16)
    lower = (right - upper.astype(jnp.float32)).astype(jnp.bfloat16)
    return jnp.dot(left, upper, preferred_element_type=jnp.float32) + jnp.dot(
        left, lower, preferred_element_type=jnp.float32
    )


def split_left(left, right):
    upper = left.astype(jnp.bfloat16)
    lower = (left - upper.astype(jnp.float32)).astype(jnp.bfloat16)
    return jnp.dot(upper, right, preferred_element_type=jnp.float32) + jnp.dot(
        lower, right, preferred_element_type=jnp.float32
    )


def shards(
    latents,
    cotangent,
    w_send,
    w_recv,
    bias,
    w_out,
    fine_sender,
    fine_receiver,
    fine_valid,
    send_rows,
    coarse_slot,
    coarse_receiver,
    coarse_valid,
):
    node_rows = latents.shape[0]
    peer_count = lax.axis_size("nodes")
    slot_count = peer_count * COARSE_CAP
    padded = extended_2(latents, (("nodes", 0),), HALO)
    outgoing = send_rows[0].reshape(-1)
    arrived = lax.all_to_all(latents[outgoing], "nodes", split_axis=0, concat_axis=0, tiled=True)
    fine_count = fine_sender.shape[0]
    senders = jnp.concatenate([padded[fine_sender], arrived[coarse_slot]], 0)
    local_recv = jnp.concatenate([fine_receiver, coarse_receiver])
    live_mask = jnp.concatenate([fine_valid, coarse_valid])
    receivers = latents[local_recv]
    preact = (
        jnp.dot(senders, w_send, preferred_element_type=jnp.float32)
        + jnp.dot(receivers, w_recv, preferred_element_type=jnp.float32)
        + bias
    )
    hidden = jax.nn.silu(preact).astype(jnp.bfloat16)
    upstream = cotangent[local_recv] * live_mask[:, None].astype(jnp.bfloat16)
    backed = jnp.dot(upstream, w_out.T, preferred_element_type=jnp.float32)
    sigmoid_pre = jax.nn.sigmoid(preact)
    grad_pre = (backed * sigmoid_pre * (1.0 + preact * (1.0 - sigmoid_pre))).astype(jnp.bfloat16)
    grad_out = jnp.dot(hidden.T, upstream, preferred_element_type=jnp.float32)
    grad_send = jnp.dot(senders.T, grad_pre, preferred_element_type=jnp.float32)
    grad_recv = jnp.dot(receivers.T, grad_pre, preferred_element_type=jnp.float32)
    grad_bias = jnp.sum(grad_pre.astype(jnp.float32), 0)
    pad_rows = padded.shape[0]
    pad_sum = jnp.dot(
        one_hot_rows(pad_rows, fine_sender, jnp.bfloat16),
        grad_pre[:fine_count],
        preferred_element_type=jnp.float32,
    )
    slot_sum = jnp.dot(
        one_hot_rows(slot_count, coarse_slot, jnp.bfloat16),
        grad_pre[fine_count:],
        preferred_element_type=jnp.float32,
    )
    node_sum = jnp.dot(
        one_hot_rows(node_rows, local_recv, jnp.bfloat16),
        grad_pre,
        preferred_element_type=jnp.float32,
    )
    send_trans = w_send.T
    pad_part = split_left(pad_sum, send_trans)
    slot_part = split_left(slot_sum, send_trans)
    local_part = split_left(node_sum, w_recv.T) + pad_part[HALO : HALO + node_rows]
    rim_part = jnp.concatenate([pad_part[:HALO], pad_part[HALO + node_rows :]], 0)
    extended = extended_2(rim_part, (("nodes", 0),), HALO)
    local_part = jnp.concatenate(
        [
            local_part[:HALO] + extended[:HALO],
            local_part[HALO : node_rows - HALO],
            local_part[node_rows - HALO :] + extended[3 * HALO :],
        ],
        0,
    )
    returned = lax.all_to_all(
        slot_part.astype(jnp.bfloat16), "nodes", split_axis=0, concat_axis=0, tiled=True
    ).astype(slot_part.dtype)
    coarse_back = split_right(one_hot_rows(COARSE_NODES, outgoing, jnp.bfloat16), returned)
    local_part = jnp.concatenate(
        [local_part[:COARSE_NODES] + coarse_back, local_part[COARSE_NODES:]], 0
    )
    local_part = lax.psum_scatter(local_part, "hid", scatter_dimension=1, tiled=True)
    columns = local_part.shape[1]
    own_part = lax.dynamic_slice_in_dim(
        cotangent, lax.axis_index("hid") * columns, columns, 1
    ).astype(jnp.float32)
    grad_nodes = local_part + own_part
    grad_send, grad_recv, grad_out, grad_bias = (
        lax.psum_scatter(grad_send, "nodes", scatter_dimension=0, tiled=True),
        lax.psum_scatter(grad_recv, "nodes", scatter_dimension=0, tiled=True),
        lax.psum_scatter(grad_out, "nodes", scatter_dimension=1, tiled=True),
        lax.psum_scatter(grad_bias, "nodes", scatter_dimension=0, tiled=True),
    )
    return (grad_nodes, grad_send, grad_recv, grad_out, grad_bias)


def solution(mesh):
    return jax.shard_map(
        shards,
        mesh=mesh,
        in_specs=(
            P("nodes", None),
            P("nodes", None),
            P(None, "hid"),
            P(None, "hid"),
            P("hid"),
            P("hid", None),
            P("nodes"),
            P("nodes"),
            P("nodes"),
            P("nodes", None, None),
            P("nodes"),
            P("nodes"),
            P("nodes"),
        ),
        out_specs=(
            P("nodes", "hid"),
            P("nodes", "hid"),
            P("nodes", "hid"),
            P("hid", "nodes"),
            P(("hid", "nodes")),
        ),
        check_vma=False,
    )
```

profile of v0, /device:TPU:1, one launch (start us, length us, event | category | flops | bytes accessed | tf_op | source)
XLA Modules:
  0.0 306.8 jit_solution(3976919043330441789)
XLA Ops:
  8.0 0.0 copy-start
  8.0 0.0 copy-start.1
  8.1 1.0 fusion.33
  9.1 4.5 %collective-permute-start = (bf16[64,512]{1,0:T(8,128)(2,1)S(1)}, bf16[64,512]{1,0:T(8,128)(2,1)S(1)}, u32[]{:S(2)}, u32[]{:S(2)}) collective-permute-start(bf16[64,512]{1,0:T(8,128)(2,1)S(1)} %get-tuple-element.27), channel_id=1, source_target_pairs={{0,8},{8,16},{16,24},{24,32},{32,40},{40,48},{48,56},{56,64},{64,7... | collective-permute-start | bytes 196616 | tf_op jit(solution)/shard_map/ppermute | solution.py:16
  13.6 5.6 %collective-permute-start.1 = (bf16[64,512]{1,0:T(8,128)(2,1)S(1)}, bf16[64,512]{1,0:T(8,128)(2,1)S(1)}, u32[]{:S(2)}, u32[]{:S(2)}) collective-permute-start(bf16[64,512]{1,0:T(8,128)(2,1)S(1)} %get-tuple-element.28), channel_id=1, source_target_pairs={{8,0},{16,8},{24,16},{32,24},{40,32},{48,40},{56,48},{64,56},{72,6... | collective-permute-start | bytes 196616 | tf_op jit(solution)/shard_map/ppermute | solution.py:19
  19.2 0.8 copy.22
  19.9 0.1 reshape_squeeze.3
  20.1 2.2 gather_fusion.2
  22.3 0.8 all_to_all.16
  23.0 11.1 %all-to-all-start = ((bf16[64,4,512]{2,1,0:T(4,128)(2,1)}), bf16[64,4,512]{2,1,0:T(4,128)(2,1)S(1)}, u32[]{:S(2)}, u32[]{:S(2)}) async-start(bf16[64,4,512]{2,1,0:T(4,128)(2,1)} %all_to_all.16), calls=%async_computation | async-start | bytes 524288 | tf_op jit(solution)/shard_map/all_to_all | solution.py:64
  34.3 0.1 eq.61
  34.5 0.0 copy-start.2
  34.5 9.2 %gather_fusion.4 = bf16[2048,512]{1,0:T(8,128)(2,1)} fusion(bf16[256,512]{1,0:T(8,128)(2,1)S(1)} %copy-done.1, s32[2048]{0:T(1024)S(1)} %broadcast_clamp_fusion), kind=kCustom, calls=%fused_computation.4 | custom fusion | bytes 4202496 | tf_op jit(solution)/shard_map/gather | solution.py:69
  43.7 9.2 %gather_fusion = bf16[2048,512]{1,0:T(8,128)(2,1)} fusion(bf16[256,512]{1,0:T(8,128)(2,1)S(1)} %copy-done.2, s32[2048]{0:T(1024)S(1)} %broadcast_clamp_fusion), kind=kCustom, calls=%fused_computation | custom fusion | bytes 4202496 | tf_op jit(solution)/shard_map/gather | solution.py:76
  52.8 0.0 collective-permute-done
  52.9 0.0 collective-permute-done.1
  52.9 5.4 %gather_fusion.1 = bf16[1536,512]{1,0:T(8,128)(2,1)} fusion(bf16[384,512]{1,0:T(8,128)(2,1)S(1)} %pad_maximum_fusion.2, s32[2048]{0:T(1024)S(1)} %pad_clamp_fusion), kind=kCustom, calls=%fused_computation.1 | custom fusion | bytes 3151872 | tf_op jit(solution)/shard_map/gather | solution.py:66
  58.3 1.5 constant_dynamic-update-slice_fusion.1
  59.8 0.0 all-to-all-done
  59.8 0.1 all_to_all.18
  59.9 2.0 gather_fusion.3
  62.0 0.0 copy-start.6
  62.0 0.0 copy-start.14
  62.0 0.7 fusion.34
  62.7 0.8 copy-done.3
  63.6 0.8 fusion
  64.3 0.8 copy-done.7
  65.1 2.3 fusion.5
  67.4 1.4 convert_reduce_fusion
  68.8 1.5 fusion.36
  70.3 1.5 fusion.35
  71.9 1.3 fusion.16
  73.2 1.6 fusion.3
  74.8 0.4 fusion.4
  75.2 0.3 fusion.23
  75.5 0.3 fusion.9
  75.8 0.8 all_to_all.19
  76.5 10.3 %all-to-all-start.1 = ((bf16[64,4,512]{2,1,0:T(4,128)(2,1)}), bf16[64,4,512]{2,1,0:T(4,128)(2,1)S(1)}, u32[]{:S(2)}, u32[]{:S(2)}) async-start(bf16[64,4,512]{2,1,0:T(4,128)(2,1)} %all_to_all.19), calls=%async_computation.1 | async-start | bytes 524288 | tf_op jit(solution)/shard_map/all_to_all | solution.py:114
  86.8 0.0 all-reduce.7.cloned.1.call-start
  86.9 0.3 fusion.26
  87.1 0.3 fusion.20
  87.4 0.3 convolution_add_fusion.1
  87.8 3.5 %collective-permute-start.2 = (f32[64,512]{1,0:T(8,128)S(1)}, f32[64,512]{1,0:T(8,128)S(1)}, u32[]{:S(2)}, u32[]{:S(2)}) collective-permute-start(f32[64,512]{1,0:T(8,128)S(1)} %get-tuple-element.23), channel_id=1, source_target_pairs={{0,8},{8,16},{16,24},{24,32},{32,40},{40,48},{48,56},{56,64},{64,7... | collective-permute-start | bytes 393224 | tf_op jit(solution)/shard_map/ppermute | solution.py:16
  91.3 1.9 collective-permute-start.3
  93.3 0.3 fusion.8
  93.6 0.0 all-reduce.7.cloned.1.call-update
  93.6 0.0 reduce-scatter.4.cloned.1.call-start
  93.6 0.7 collective-permute-done.2
  94.3 3.9 %collective-permute-done.3 = f32[64,512]{1,0:T(8,128)S(1)} collective-permute-done((f32[64,512]{1,0:T(8,128)S(1)}, f32[64,512]{1,0:T(8,128)S(1)}, u32[]{:S(2)}, u32[]{:S(2)}) %collective-permute-start.3) | collective-permute-done | bytes 131104 | tf_op jit(solution)/shard_map/ppermute | solution.py:19
  98.2 1.8 all-to-all-done.1
  100.0 0.1 all_to_all.21
  100.1 0.1 fusion.28
  100.2 0.2 slice_add_fusion.2
  100.4 1.0 copy.25
  101.4 0.0 reduce-scatter.4.cloned.1.call-update
  101.4 1.3 dynamic-slice
  104.0 123.8 %all-reduce.3 = f32[256]{0:T(256)S(1)} all-reduce(f32[256]{0:T(256)S(1)} %get-tuple-element.29), channel_id=6, replica_groups=mesh['nodes'=64,'hid'=8] {'nodes'}, use_global_device_ids=true, to_apply=%region_5.6.clone | all-reduce | flops 256 | bytes 2048
  227.8 0.6 dynamic-slice.7
  228.4 66.5 %all-reduce.7.cloned.1.call-done = (f32[512,256]{1,0:T(8,128)}, f32[512,256]{1,0:T(8,128)}, f32[256,512]{0,1:T(8,128)}) async-done(((f32[512,256]{1,0:T(8,128)}, f32[512,256]{1,0:T(8,128)}, f32[256,512]{0,1:T(8,128)}), (f32[512,256]{1,0:T(8,128)}, f32[512,256]{1,0:T(8,128)}, f32[256,512]{0,1:T(8,128)})) %all-reduce.7.cloned.1.call-update) | async-done | bytes 1572880
  295.0 1.3 constant_dynamic-slice_fusion
  296.2 1.3 constant_dynamic-slice_fusion.1
  297.6 0.9 copy.26
  298.5 0.1 convert_add_fusion
  298.6 0.7 copy.24
  (45 shorter events, 0.3 us)
Async XLA Ops:
  8.0 53.9 %copy-start = (bf16[512,256]{1,0:T(8,128)(2,1)S(1)}, bf16[512,256]{1,0:T(8,128)(2,1)}, u32[]{:S(2)}) copy-start(bf16[512,256]{1,0:T(8,128)(2,1)} %param.15) | copy-start | bytes 786436
  8.0 26.5 %copy-start.1 = (bf16[256,512]{1,0:T(8,128)(2,1)S(1)}, bf16[256,512]{1,0:T(8,128)(2,1)}, u32[]{:S(2)}) copy-start(bf16[256,512]{1,0:T(8,128)(2,1)} %param.13) | copy-start | bytes 786436
  8.0 26.2 %copy-start.13 = (s32[512]{0:T(512)S(1)}, s32[512]{0:T(512)}, u32[]{:S(2)}) copy-start(s32[512]{0:T(512)} %param.23) | copy-start | bytes 6148
  8.0 26.2 %copy-start.8 = (s32[1536]{0:T(1024)S(1)}, s32[1536]{0:T(1024)}, u32[]{:S(2)}) copy-start(s32[1536]{0:T(1024)} %param.20) | copy-start | bytes 18436
  8.0 26.2 %copy-start.11 = (s32[512]{0:T(512)S(1)}, s32[512]{0:T(512)}, u32[]{:S(2)}) copy-start(s32[512]{0:T(512)} %param.24) | copy-start | bytes 6148
  8.1 26.2 %copy-start.10 = (s32[1536]{0:T(1024)S(1)}, s32[1536]{0:T(1024)}, u32[]{:S(2)}) copy-start(s32[1536]{0:T(1024)} %param.19) | copy-start | bytes 18436
  8.1 26.4 %copy-start.12 = (s32[512]{0:T(512)S(1)}, s32[512]{0:T(512)}, u32[]{:S(2)}) copy-start(s32[512]{0:T(512)} %param.25) | copy-start | bytes 6148
  8.1 26.4 %copy-start.9 = (s32[1536]{0:T(1024)S(1)}, s32[1536]{0:T(1024)}, u32[]{:S(2)}) copy-start(s32[1536]{0:T(1024)} %param.21) | copy-start | bytes 18436
  9.1 43.8 %collective-permute-start = (bf16[64,512]{1,0:T(8,128)(2,1)S(1)}, bf16[64,512]{1,0:T(8,128)(2,1)S(1)}, u32[]{:S(2)}, u32[]{:S(2)}) collective-permute-start(bf16[64,512]{1,0:T(8,128)(2,1)S(1)} %get-tuple-element.27), channel_id=1, source_target_pairs={{0,8},{8,16},{16,24},{24,32},{32,40},{40,48},{48,56},{56,64},{64,7... | collective-permute-start | bytes 196616 | tf_op jit(solution)/shard_map/ppermute | solution.py:16
  13.6 39.3 %collective-permute-start.1 = (bf16[64,512]{1,0:T(8,128)(2,1)S(1)}, bf16[64,512]{1,0:T(8,128)(2,1)S(1)}, u32[]{:S(2)}, u32[]{:S(2)}) collective-permute-start(bf16[64,512]{1,0:T(8,128)(2,1)S(1)} %get-tuple-element.28), channel_id=1, source_target_pairs={{8,0},{16,8},{24,16},{32,24},{40,32},{48,40},{56,48},{64,56},{72,6... | collective-permute-start | bytes 196616 | tf_op jit(solution)/shard_map/ppermute | solution.py:19
  23.0 36.8 %all-to-all-start = ((bf16[64,4,512]{2,1,0:T(4,128)(2,1)}), bf16[64,4,512]{2,1,0:T(4,128)(2,1)S(1)}, u32[]{:S(2)}, u32[]{:S(2)}) async-start(bf16[64,4,512]{2,1,0:T(4,128)(2,1)} %all_to_all.16), calls=%async_computation | async-start | bytes 524288 | tf_op jit(solution)/shard_map/all_to_all | solution.py:64
  34.5 9.2 %copy-start.2 = (bf16[256,512]{1,0:T(8,128)(2,1)S(1)}, bf16[256,512]{1,0:T(8,128)(2,1)}, u32[]{:S(2)}) copy-start(bf16[256,512]{1,0:T(8,128)(2,1)} %param.14) | copy-start | bytes 786436
  62.0 1.6 copy-start.3
  62.0 1.6 copy-start.6
  62.0 1.6 copy-start.14
  63.5 1.6 copy-start.7
  65.1 2.3 copy-start.15
  68.8 1.6 copy-start.4
  71.9 2.9 copy-start.5
  76.5 23.5 %all-to-all-start.1 = ((bf16[64,4,512]{2,1,0:T(4,128)(2,1)}), bf16[64,4,512]{2,1,0:T(4,128)(2,1)S(1)}, u32[]{:S(2)}, u32[]{:S(2)}) async-start(bf16[64,4,512]{2,1,0:T(4,128)(2,1)} %all_to_all.19), calls=%async_computation.1 | async-start | bytes 524288 | tf_op jit(solution)/shard_map/all_to_all | solution.py:114
  86.8 208.1 %all-reduce.7.cloned.1.call-start = ((), (), s32[]{:S(2)}) async-start(), calls=%async_computation.4 | async-start | bytes 3145728
  87.8 6.5 %collective-permute-start.2 = (f32[64,512]{1,0:T(8,128)S(1)}, f32[64,512]{1,0:T(8,128)S(1)}, u32[]{:S(2)}, u32[]{:S(2)}) collective-permute-start(f32[64,512]{1,0:T(8,128)S(1)} %get-tuple-element.23), channel_id=1, source_target_pairs={{0,8},{8,16},{16,24},{24,32},{32,40},{40,48},{48,56},{56,64},{64,7... | collective-permute-start | bytes 393224 | tf_op jit(solution)/shard_map/ppermute | solution.py:16
  91.3 6.9 %collective-permute-start.3 = (f32[64,512]{1,0:T(8,128)S(1)}, f32[64,512]{1,0:T(8,128)S(1)}, u32[]{:S(2)}, u32[]{:S(2)}) collective-permute-start(f32[64,512]{1,0:T(8,128)S(1)} %get-tuple-element.24), channel_id=1, source_target_pairs={{8,0},{16,8},{24,16},{32,24},{40,32},{48,40},{56,48},{64,56},{72,6... | collective-permute-start | bytes 393224 | tf_op jit(solution)/shard_map/ppermute | solution.py:19
  93.6 204.0 %reduce-scatter.4.cloned.1.call-start = ((), (), s32[]{:S(2)}) async-start(), calls=%async_computation.3 | async-start | bytes 589824
Sparse Core Ops, SparseCore 0:
  93.7 201.1 all-reduce.6
Sparse Core Ops, SparseCore 1:
  101.5 35.5 reduce-scatter.3
where the time goes:
time: 308 us; the launch traced here: 307 us
  blocking collectives  124 us (40%)
  waiting for transfers between devices  72.9 us (24%)
  local copies, waits for them, and re-layouts  41.9 us (14%)
  starting transfers between devices  37.1 us (12%)
  between operations  17.3 us (6%)
  matrix products  13.5 us (4%)
    unnamed x1, blocking collectives  124 us
    unnamed x4, waiting for transfers between devices  66.6 us
    all_to_all x1, starting transfers between devices, shards(): lax.all_to_all(latents[outgoing], 'nodes', split_axis=0, concat_axis=0, t...  11.1 us
    unnamed x41, local copies, waits for them, and re-layouts  11.1 us
    all_to_all x1, starting transfers between devices, shards(): lax.all_to_all(slot_part.astype(jnp.bfloat16), 'nodes', split_axis=0, con...  10.3 us
    gather x1, local copies, waits for them, and re-layouts, shards(): receivers = latents[local_recv]  9.16 us
    gather x1, local copies, waits for them, and re-layouts, shards(): upstream = cotangent[local_recv] * live_mask[:, None].astype(jnp.bfloat16)  9.16 us
    ppermute x2, starting transfers between devices, extended_2(): lax.ppermute(lax.slice_in_dim(block, block.shape[dim] - width, None, axis...  8.05 us
  transfers between devices with their start and end apart: 8, of which 4 were waited for; matrix products, arithmetic and copies ran while one was open for 12% of the time, Pallas kernels for 0%

commit v1 on v0

v1 whole, which is shorter than its diff:
```python
import jax
import jax.numpy as jnp
from jax import lax
from jax.experimental import pallas as pl
from jax.experimental.pallas import tpu as pltpu
from jax.sharding import PartitionSpec as P

BF = jnp.bfloat16
F32 = jnp.float32
MESH = pl.DeviceIdType.MESH
NODES = 64
HID = 8
ZS, XS = 8, 4
ROWS = 256
D = 512
H = 256
HALO = 64
FINE = 1536
COARSE = 512
CH = 512
TILES = (8, 9, 8)


def nn(a, b):
    return lax.dot_general(a, b, (((1,), (0,)), ((), ())), preferred_element_type=F32)


def nt(a, b):
    return lax.dot_general(a, b, (((1,), (1,)), ((), ())), preferred_element_type=F32)


def split(v):
    hi = v.astype(BF)
    return hi, (v - hi.astype(F32)).astype(BF)


def one_hot(count, row):
    return (lax.broadcasted_iota(jnp.int32, (count, row.shape[1]), 0) == row).astype(F32).astype(BF)


def eye(n):
    a = lax.broadcasted_iota(jnp.int32, (n, n), 0)
    b = lax.broadcasted_iota(jnp.int32, (n, n), 1)
    return (a == b).astype(F32).astype(BF)


def kernel(
    lat_h, cot_h, ws_h, wr_h, bias_h, wo_h, fs_h, fr_h, fv_h, sr_h, cs_h, cr_h, cv_h,
    rz0, rz1, rz2, own_h, node_h, rcy,
    low, lat, cot, ws, wr, bias, wo, fs, fr, fv, sr, cs, cr, cv, load_sem,
    msg32, zrow, zrow32, zraw, zraw32, pick_s, pick_t, psel, prow, praw_s, praw_r, halo, wst, latt, cott, a_src, a_rcv, a_slot,
    g_src, g_rh, g_slot,
    ret_s, ret_r, col_s, col_r, rim_s, rim_r,
    buf0, buf1, buf2, rc0, rc1, rc2, xs0, xs1, xs2, rx0, rx1, rx2, sums, own, zs0, zs1, zs2,
    part, ys, ry, node_v, cy,
    zg_sem, pg_sem, zr_sem, pr_sem, halo_sem, rp_sem, rz_sem, rim_sem, core_sem, x_sem, z_sem, y_sem, cy_sem, out_sem,
):
    b = lax.axis_index("nodes")
    y = lax.axis_index("hid")
    c = lax.rem(b, 2)
    x = lax.rem(b // 2, XS)
    z = b // (2 * XS)
    bar = pltpu.get_barrier_semaphore()

    loads = [
        pltpu.make_async_copy(src, dst, load_sem.at[i])
        for i, (src, dst) in enumerate(
            (
                (sr_h, sr), (ws_h, ws), (lat_h, lat), (wr_h, wr), (cot_h, cot), (wo_h, wo), (bias_h, bias),
                (fs_h, fs), (fr_h, fr), (fv_h, fv), (cs_h, cs), (cr_h, cr), (cv_h, cv),
            )
        )
    ]
    first = pltpu.make_async_copy(lat_h.at[0:16], low, load_sem.at[13])
    first.start()
    for load in loads[0:2]:
        load.start()

    def block(zz, xx, cc):
        return (zz * XS + xx) * 2 + cc

    def plane(m, sign):
        return block(z, lax.rem(x + XS + sign * (m // 2), XS), lax.rem(c + m % 2, 2))

    def column(k, sign):
        return block(lax.rem(z + ZS + sign * k, ZS), x, c)

    def greet(**device):
        pl.semaphore_signal(bar, inc=1, device_id=device, device_id_type=MESH)

    for k in (4, 3, 5, 2, 6, 1, 7):
        greet(nodes=column(k, 1))
    for m in (4, 5, 2, 3, 6, 7, 1):
        greet(nodes=plane(m, 1))
    greet(nodes=lax.rem(b + NODES - 1 + 2 * c, NODES))
    for k in (4, 3, 5, 2, 6, 1, 7):
        greet(hid=lax.rem(y + k, HID))
    for load in loads[2:]:
        load.start()

    def remote(src, dst, sems, at, **device):
        return pltpu.make_async_remote_copy(
            src_ref=src, dst_ref=dst, send_sem=sems.at[0, at], recv_sem=sems.at[1, at],
            device_id=device, device_id_type=MESH,
        )

    msg32[...] = jnp.zeros_like(msg32)
    loads[0].wait()
    msg32[16:20, 0:NODES] = sr[...].astype(F32)
    first.wait()
    low32 = low[...].astype(F32)
    for k in range(4):
        zraw32[0, 8 * k : 8 * k + 8, :] = low32[0:8, 128 * k : 128 * k + 128]
    zraw[0] = zraw32[0].astype(BF)
    loads[1].wait()
    ahead = nn(low[...], ws[...])
    for k in range(2):
        msg32[8 * k : 8 * k + 8, :] = ahead[0:8, 128 * k : 128 * k + 128]
    zrow[0] = msg32[...].astype(BF)

    pl.semaphore_wait(bar, 22)

    z_rows = [remote(zrow.at[0], zrow.at[k], zg_sem, k - 1, nodes=column(k, 1)) for k in (4, 3, 5, 2, 6, 1, 7)]
    for copy in z_rows:
        copy.start()
    loads[2].wait()
    up = lax.rem(b + 1, NODES)
    down = lax.rem(b + NODES - 1, NODES)
    halos = (
        remote(lat.at[ROWS - HALO : ROWS], halo.at[0:HALO], halo_sem, 0, nodes=up),
        remote(lat.at[0:HALO], halo.at[HALO : 2 * HALO], halo_sem, 1, nodes=down),
    )
    for copy in halos:
        copy.start()

    z_raws = [remote(zraw.at[0], zraw.at[k], zr_sem, k - 1, nodes=column(k, 1)) for k in (4, 3, 5, 2, 6, 1, 7)]
    for copy in z_raws:
        copy.start()

    for load in loads[3:]:
        load.wait()
    eye256 = eye(256)
    wst[...] = nt(eye256, ws[...]).astype(BF)
    wrt = nt(eye256, wr[...]).astype(BF)
    bias_row = bias[...]
    b0 = bias_row.astype(BF)
    rest = bias_row - b0.astype(F32)
    b1 = rest.astype(BF)
    b2 = (rest - b1.astype(F32)).astype(BF)
    b_rows = jnp.concatenate([b0.astype(F32), b1.astype(F32), b2.astype(F32), jnp.zeros((5, H), F32)], 0)
    bias_col = jnp.sum(nt(eye256, b_rows.astype(BF)), axis=1, keepdims=True)
    for k in range(2):
        latt[256 * k : 256 * k + 256, 0:ROWS] = nt(eye256, lat[:, 256 * k : 256 * k + 256]).astype(BF)
        cott[256 * k : 256 * k + 256, :] = nt(eye256, cot[:, 256 * k : 256 * k + 256]).astype(BF)
    hi, lo = split(nn(wst[...], latt[:, 0:ROWS]))
    a_src[0:H, 0:ROWS] = hi
    a_src[H : 2 * H, 0:ROWS] = lo
    hi, lo = split(nn(wrt, latt[:, 0:ROWS]) + bias_col)
    a_rcv[0:H, :] = hi
    a_rcv[H : 2 * H, :] = lo
    a_rcv[2 * H : 3 * H, :] = nt(wo[...], cot[...]).astype(BF)

    wide = lax.broadcasted_iota(jnp.int32, (256, 128), 0)
    lane = lax.broadcasted_iota(jnp.int32, (256, 128), 1)
    spread = (lane == (wide & 7) * 16 + ((wide >> 3) & 3)).astype(F32).astype(BF)
    asked = ((z * XS + ((x + (wide >> 6)) & (XS - 1))) << 1) + ((c + (wide >> 5)) & 1)
    here = lane == asked
    for copy in z_rows:
        copy.wait()
    zrow32[...] = zrow[...].astype(F32)
    table = zrow32[:, 16:32, :].reshape(ZS * 16, 128).astype(BF)
    wanted = jnp.sum(jnp.where(here, nn(spread, table), 0.0), axis=1, keepdims=True)
    tall = lax.broadcasted_iota(jnp.int32, (256, 64), 0)
    node = lax.broadcasted_iota(jnp.int32, (256, 64), 1)
    chosen = ((node >> 3) == (tall & 7)) & ((node & 7).astype(F32) == wanted)
    pick_s[...] = chosen.astype(F32).astype(BF)
    for k in range(2):
        rows = zrow32[:, 8 * k : 8 * k + 8, :].reshape(64, 128).astype(BF)
        psel[:, :, 128 * k : 128 * k + 128] = nn(pick_s[...], rows).astype(BF).reshape(8, 32, 128)
    p_rows = [remote(psel.at[m], prow.at[m], pg_sem, m - 1, nodes=plane(m, 1)) for m in (4, 5, 2, 3, 6, 7, 1)]
    for copy in p_rows:
        copy.start()
    prow[0] = psel[0]
    pick_t[...] = nt(eye(64), pick_s[...]).astype(BF)

    for copy in halos:
        copy.wait()
    row = lax.broadcasted_iota(jnp.int32, (2 * HALO, D), 0)
    outside = ((row < HALO) & (b == 0)) | ((row >= HALO) & (b == NODES - 1))
    rim = jnp.where(outside, 0.0, halo[...].astype(F32)).astype(BF)
    for k in range(2):
        latt[256 * k : 256 * k + 256, ROWS : ROWS + 2 * HALO] = nt(eye256, rim[:, 256 * k : 256 * k + 256]).astype(BF)
    hi, lo = split(nn(wst[...], latt[:, ROWS : ROWS + 2 * HALO]))
    a_src[0:H, ROWS : ROWS + 2 * HALO] = hi
    a_src[H : 2 * H, ROWS : ROWS + 2 * HALO] = lo

    def edges(source, send_row, recv_row, live_row, count, exact):
        pick_s = one_hot(count, send_row)
        pick_r = one_hot(ROWS, recv_row)
        from_s = nn(source[...], pick_s)
        from_r = nn(a_rcv[...], pick_r)
        live = live_row.astype(F32)
        pre = from_s[0:H] + from_r[0:H] + from_r[H : 2 * H]
        if exact:
            pre += from_s[H : 2 * H]
        sig = 0.5 + 0.5 * jnp.tanh(0.5 * pre)
        act = pre * sig
        slope = sig + act * (1.0 - sig)
        grad = (from_r[2 * H :] * live * slope).astype(BF)
        hidden = (act * live).astype(BF)
        return pick_s, pick_r, grad, hidden

    for k in range(FINE // CH):
        at = slice(k * CH, (k + 1) * CH)
        s = fs[at].reshape(1, CH)
        s = jnp.where(s < HALO, s + ROWS, jnp.where(s < HALO + ROWS, s - HALO, s))
        by_s, by_r, grad, hidden = edges(a_src, s, fr[at].reshape(1, CH), fv[at].reshape(1, CH), ROWS + 2 * HALO, True)
        add_s, add_r = nt(by_s, grad), nt(by_r, jnp.concatenate([grad, hidden], 0))
        if k == 0:
            g_src[...] = add_s
            g_rh[...] = add_r
        else:
            g_src[...] += add_s
            g_rh[...] += add_r
        if k == 0:
            for copy in z_raws:
                copy.wait()
            zraw32[...] = zraw[...].astype(F32)
            for i in range(4):
                rows = zraw32[:, 8 * i : 8 * i + 8, :].reshape(64, 128).astype(BF)
                praw_s[:, :, 128 * i : 128 * i + 128] = nn(pick_s[...], rows).astype(BF).reshape(8, 32, 128)
            p_raws = [
                remote(praw_s.at[m], praw_r.at[m], pr_sem, m - 1, nodes=plane(m, 1)) for m in (4, 5, 2, 3, 6, 7, 1)
            ]
            for copy in p_raws:
                copy.start()
            praw_r[0] = praw_s[0]

    rim_s[...] = g_src[ROWS : ROWS + 2 * HALO, :].astype(BF)
    rims = (
        remote(rim_s.at[0:HALO], rim_r.at[HALO : 2 * HALO], rim_sem, 0, nodes=down),
        remote(rim_s.at[HALO : 2 * HALO], rim_r.at[0:HALO], rim_sem, 1, nodes=up),
    )
    for copy in rims:
        copy.start()

    for copy in p_rows:
        copy.wait()
    a_slot[...] = nt(eye256, prow[...].reshape(256, H)).astype(BF)
    q = cs[...]
    place = (
        (((x + XS - ((q >> 3) & (XS - 1))) & (XS - 1)) << 6)
        + (((c + (q >> 2)) & 1) << 5)
        + ((q & 3) << 3)
        + ((z + ZS - (q >> 5)) & (ZS - 1))
    )
    by_s, by_r, grad, hidden = edges(a_slot, place, cr[...], cv[...], 256, False)

    bufs, rcs, xss, rxs = (buf0, buf1, buf2), (rc0, rc1, rc2), (xs0, xs1, xs2), (rx0, rx1, rx2)
    zss, rzs = (zs0, zs1, zs2), (rz0, rz1, rz2)

    def lay_out(buf, value):
        for d in range(NODES):
            piece = value[8 * d : 8 * d + 8, :]
            tile = jnp.concatenate([piece[:, 0:128], piece[:, 128:256]], 0)
            buf[d % 2, (d // 2) % XS, d // (2 * XS)] = tile.astype(BF)

    cores = []

    def send_core(a):
        copy = remote(bufs[a].at[1 - c], rcs[a], core_sem, a, nodes=b + 1 - 2 * c)
        copy.start()
        cores.append(copy)

    x_copies = []

    def send_x(a):
        cores[a].wait()
        xss[a][...] = (bufs[a][c].astype(F32) + rcs[a][...].astype(F32)).astype(BF)
        for k in (2, 1, 3):
            to = lax.rem(x + k, XS)
            copy = remote(
                xss[a].at[to], rxs[a].at[k - 1], x_sem, 3 * a + k - 1, nodes=(z * XS + to) * 2 + c
            )
            copy.start()
            x_copies.append(copy)

    lay_out(buf0, nn(cott[...], (g_rh[:, H : 2 * H] + nt(by_r, hidden)).astype(BF)))
    send_core(0)

    g_slot[...] = nt(by_s, grad).astype(BF)
    ret_s[...] = g_slot[...].reshape(8, 32, H)
    backs = [remote(ret_s.at[m], ret_r.at[m], rp_sem, m - 1, nodes=plane(m, -1)) for m in (4, 5, 2, 3, 6, 7, 1)]
    for copy in backs:
        copy.start()
    ret_r[0] = ret_s[0]

    g_recv = g_rh[:, 0:H] + nt(by_r, grad)
    lay_out(buf1, nn(latt[:, 0:ROWS], g_recv.astype(BF)))
    total = jnp.sum(g_recv, axis=0, keepdims=True)
    bias_tile = jnp.concatenate([total[:, 0:128], total[:, 128:256], jnp.zeros((14, 128), F32)], 0).astype(BF)
    for i in range(2):
        for k in range(XS):
            buf1[i, k, 8] = bias_tile
    send_core(1)
    send_x(0)
    for copy in p_raws:
        copy.wait()
    arr = praw_r[...].reshape(256, D)
    for k in range(2):
        latt[256 * k : 256 * k + 256, 384:640] = nt(eye256, arr[:, 256 * k : 256 * k + 256]).astype(BF)
    lay_out(
        buf2,
        nn(latt[:, 0 : ROWS + 2 * HALO], g_src[...].astype(BF)) + nn(latt[:, 384:640], g_slot[...]),
    )
    send_core(2)
    send_x(1)

    for copy in rims:
        copy.wait()
    low = jnp.where(b == 0, 0.0, rim_r[0:HALO, :].astype(F32))
    high = jnp.where(b == NODES - 1, 0.0, rim_r[HALO : 2 * HALO, :].astype(F32))
    g_src[0:HALO, :] += low
    g_src[ROWS - HALO : ROWS, :] += high
    node = nt(ws[...], g_src[0:ROWS, :].astype(BF)) + nt(wr[...], g_recv.astype(BF))
    part[...] = node.reshape(HID, 64, ROWS)
    ys[...] = node.astype(BF).reshape(HID, 64, ROWS)
    y_copies = []
    for k in (4, 3, 5, 2, 6, 1, 7):
        to = lax.rem(y + k, HID)
        copy = remote(ys.at[to], ry.at[k - 1], y_sem, k - 1, hid=to)
        copy.start()
        y_copies.append(copy)

    send_x(2)

    for copy in backs:
        copy.wait()
    col_s[...] = nn(pick_t[...], ret_r[...].reshape(256, H)).reshape(ZS, 8, H)
    cols = [remote(col_s.at[k], col_r.at[k], rz_sem, k - 1, nodes=column(k, -1)) for k in (4, 3, 5, 2, 6, 1, 7)]
    for copy in cols:
        copy.start()
    col_r[0] = col_s[0]

    z_copies = []
    for a in range(3):
        for copy in x_copies[3 * a : 3 * a + 3]:
            copy.wait()
        mine = bufs[a][c, x].astype(F32) + rcs[a][x].astype(F32)
        for k in range(3):
            mine += rxs[a][k].astype(F32)
        sums[0:8] = mine[0:8]
        own[a] = sums[z]
        zss[a][:, 0:16, :] = mine[0:8].astype(BF)
        if a == 1:
            own[3] = mine[8]
            for k in range(ZS):
                zss[a][k, 16:32, :] = mine[8].astype(BF)
        for k in (4, 3, 5, 2, 6, 1, 7):
            to = lax.rem(z + k, ZS)
            copy = remote(
                zss[a].at[to], rzs[a].at[k - 1], z_sem, 7 * a + k - 1, nodes=(to * XS + x) * 2 + c
            )
            copy.start()
            z_copies.append(copy)

    own_out = pltpu.make_async_copy(own, own_h, out_sem.at[0])
    own_out.start()

    for copy in cols:
        copy.wait()
    coarse = col_r[0]
    for k in range(1, ZS):
        coarse += col_r[k]
    coarse = jnp.concatenate([coarse, jnp.zeros((8, H), F32)], 0)
    hi, lo = split(coarse)
    coarse_part = nt(hi, ws[...]) + nt(lo, ws[...])
    for k in range(HID):
        cy[k] = coarse_part[0:8, 128 * (k // 2) : 128 * (k // 2) + 128]
    cy_copies = []
    for k in (4, 3, 5, 2, 6, 1, 7):
        to = lax.rem(y + k, HID)
        copy = remote(cy.at[to], rcy.at[k - 1], cy_sem, k - 1, hid=to)
        copy.start()
        cy_copies.append(copy)

    cy_out = pltpu.make_async_copy(cy.at[y], rcy.at[HID - 1], out_sem.at[1])
    cy_out.start()

    for copy in y_copies:
        copy.wait()
    mine = part[y] + cott[pl.ds(pl.multiple_of(y * 64, 64), 64), :].astype(F32)
    for k in range(HID - 1):
        mine += ry[k].astype(F32)
    node_v[...] = mine
    node_out = pltpu.make_async_copy(node_v, node_h, out_sem.at[2])
    node_out.start()

    for copy in z_copies + cy_copies + [own_out, cy_out, node_out]:
        copy.wait()


def finish(
    rz0_h, rz1_h, rz2_h, own_h, node_h, rcy_h,
    n_out, s_out, r_out, o_out, b_out,
    rz0, rz1, rz2, own, node, rcy, n_v, s_v, r_v, o_v, in_sem, out_sem,
):
    b = lax.axis_index("nodes")
    y = lax.axis_index("hid")
    reads = [
        pltpu.make_async_copy(src, dst, in_sem.at[i])
        for i, (src, dst) in enumerate(
            ((own_h, own), (rz0_h, rz0), (rz1_h, rz1), (rz2_h, rz2), (rcy_h, rcy), (node_h, node))
        )
    ]
    for copy in reads:
        copy.start()
    writes = []

    def write(i, src, dst):
        copy = pltpu.make_async_copy(src, dst, out_sem.at[i])
        copy.start()
        writes.append(copy)

    reads[0].wait()
    for a, (rz, vec, out) in enumerate(((rz0, o_v, o_out), (rz1, r_v, r_out), (rz2, s_v, s_out))):
        reads[1 + a].wait()
        tile = own[a]
        for k in range(ZS - 1):
            tile += rz[k, 0:16].astype(F32)
        vec[...] = jnp.concatenate([tile[0:8], tile[8:16]], 1)
        write(a, vec, out)
    tile = own[3]
    for k in range(ZS - 1):
        tile += rz1[k, 16:32].astype(F32)
    line = jnp.broadcast_to(jnp.where(b < NODES // 2, tile[0:1], tile[1:2]), (8, 128))
    lane = lax.broadcasted_iota(jnp.int32, (128, 128), 0)
    want = lax.broadcasted_iota(jnp.int32, (128, 128), 1) + 4 * lax.rem(b, NODES // 2)
    take = (lane == want).astype(F32).astype(BF)
    v0 = line.astype(BF)
    rest = line - v0.astype(F32)
    v1 = rest.astype(BF)
    v2 = (rest - v1.astype(F32)).astype(BF)
    b_out[...] = (nn(v0, take) + nn(v1, take) + nn(v2, take))[0, 0:4]

    reads[4].wait()
    late = rcy[HID - 1]
    for k in range(HID - 1):
        late += rcy[k]
    late = jnp.concatenate([late, jnp.zeros((120, 128), F32)], 0).T
    late = jnp.where(lax.rem(y, 2) == 0, late[0:64, :], late[64:128, :])
    reads[5].wait()
    n_v[:, 0:128] = node[:, 0:128] + late
    n_v[:, 128:256] = node[:, 128:256]
    write(3, n_v, n_out)
    for copy in writes:
        copy.wait()


def vm(shape, dtype):
    return pltpu.VMEM(shape, dtype)


def shards(
    latents, cotangent, w_send, w_recv, bias, w_out, fine_sender, fine_receiver, fine_valid,
    send_rows, coarse_slot, coarse_receiver, coarse_valid,
):
    i32 = jnp.int32
    operands = (
        latents, cotangent, w_send, w_recv, bias.reshape(1, H), w_out,
        fine_sender, fine_receiver, fine_valid,
        send_rows[0].T,
        coarse_slot.reshape(1, COARSE), coarse_receiver.reshape(1, COARSE), coarse_valid.reshape(1, COARSE),
    )
    sems = pltpu.SemaphoreType.DMA
    scratch = [vm((16, D), BF)] + [vm(v.shape, v.dtype) for v in operands] + [sems((14,))]
    scratch += [
        vm((32, 128), F32), vm((ZS, 32, 128), BF), vm((ZS, 32, 128), F32), vm((ZS, 32, 128), BF),
        vm((ZS, 32, 128), F32), vm((256, 64), BF), vm((64, 256), BF),
        vm((8, 32, H), BF), vm((8, 32, H), BF), vm((8, 32, D), BF), vm((8, 32, D), BF),
        vm((2 * HALO, D), BF), vm((H, D), BF), vm((D, 640), BF), vm((D, ROWS), BF),
        vm((2 * H, 384), BF), vm((3 * H, ROWS), BF), vm((H, 256), BF),
        vm((384, H), F32), vm((ROWS, 2 * H), F32), vm((256, H), BF),
        vm((8, 32, H), BF), vm((8, 32, H), BF), vm((ZS, 8, H), F32), vm((ZS, 8, H), F32),
        vm((2 * HALO, H), BF), vm((2 * HALO, H), BF),
    ]
    scratch += [vm((2, XS, t, 16, 128), BF) for t in TILES]
    scratch += [vm((XS, t, 16, 128), BF) for t in TILES]
    scratch += [vm((XS, t, 16, 128), BF) for t in TILES]
    scratch += [vm((XS - 1, t, 16, 128), BF) for t in TILES]
    scratch += [vm((ZS, 16, 128), F32), vm((4, 16, 128), F32)]
    scratch += [vm((ZS, 16 * (t - 7), 128), BF) for t in TILES]
    scratch += [
        vm((HID, 64, ROWS), F32), vm((HID, 64, ROWS), BF), vm((HID - 1, 64, ROWS), BF),
        vm((64, ROWS), F32), vm((HID, 8, 128), F32),
    ]
    scratch += [
        sems((2, 7)), sems((2, 7)), sems((2, 7)), sems((2, 7)), sems((2, 2)), sems((2, 7)), sems((2, 7)), sems((2, 2)), sems((2, 3)), sems((2, 9)), sems((2, 21)),
        sems((2, 7)), sems((2, 7)), sems((3,)),
    ]
    hbm = pl.BlockSpec(memory_space=pltpu.MemorySpace.HBM)
    kept = [
        ((ZS - 1, 16, 128), BF), ((ZS - 1, 32, 128), BF), ((ZS - 1, 16, 128), BF),
        ((4, 16, 128), F32), ((64, ROWS), F32), ((HID, 8, 128), F32),
    ]
    arrived = pl.pallas_call(
        kernel,
        out_shape=[jax.ShapeDtypeStruct(shape, dtype) for shape, dtype in kept],
        in_specs=[hbm] * 13,
        out_specs=[hbm] * 6,
        scratch_shapes=scratch,
        compiler_params=pltpu.CompilerParams(
            collective_id=0, has_side_effects=True, vmem_limit_bytes=64 * 1024 * 1024
        ),
        name="edge_update",
    )(*operands)
    results = [(64, ROWS), (8, H), (8, H), (8, H)]
    out_n, out_s, out_r, out_o, out_b = pl.pallas_call(
        finish,
        out_shape=[jax.ShapeDtypeStruct(shape, F32) for shape in results + [(4,)]],
        in_specs=[hbm] * 6,
        out_specs=[hbm] * 4 + [pl.BlockSpec(memory_space=pltpu.VMEM)],
        scratch_shapes=[vm(shape, dtype) for shape, dtype in kept]
        + [vm(shape, F32) for shape in results]
        + [sems((6,)), sems((4,))],
        compiler_params=pltpu.CompilerParams(vmem_limit_bytes=64 * 1024 * 1024),
        name="finish",
    )(*arrived)
    return out_n.T, out_s, out_r, out_o.T, out_b


def solution(mesh):
    return jax.shard_map(
        shards,
        mesh=mesh,
        in_specs=(
            P("nodes", None), P("nodes", None), P(None, "hid"), P(None, "hid"), P("hid"), P("hid", None),
            P("nodes"), P("nodes"), P("nodes"), P("nodes", None, None), P("nodes"), P("nodes"), P("nodes"),
        ),
        out_specs=(
            P("nodes", "hid"), P("nodes", "hid"), P("nodes", "hid"), P("hid", "nodes"), P(("hid", "nodes")),
        ),
        check_vma=False,
    )
```

time: 308 us -> 44.3 us (0.14)
  blocking collectives: 124 us -> 0 us
  waiting for transfers between devices: 72.9 us -> 0 us
  Pallas kernels: 0 us -> 43.5 us
  local copies, waits for them, and re-layouts: 41.9 us -> 0 us
  starting transfers between devices: 37.1 us -> 0 us
  between operations: 17.3 us -> 0.64 us
  matrix products: 13.5 us -> 0 us
    unnamed x1 -> x0, blocking collectives: 124 us -> none
    unnamed x4 -> x0, waiting for transfers between devices: 66.6 us -> none
    pallas_call x0 -> x2, Pallas kernels: none -> 43.5 us  [the longest x1 41.1 us: shards(): pl.pallas_call(kernel, out_shape=[jax.ShapeDtypeStruct(shape, dtype) for...]
    gather x5 -> x0, local copies, waits for them, and re-layouts: 27.9 us -> none  [the longest x1 9.16 us: shards(): receivers = latents[local_recv]]
    all_to_all x2 -> x0, starting transfers between devices: 21.4 us -> none  [the longest x1 11.1 us: shards(): lax.all_to_all(latents[outgoing], 'nodes', split_axis=0, concat_axis=0, t...]
    ppermute x4 -> x0, starting transfers between devices: 15.5 us -> none  [the longest x2 8.05 us: extended_2(): lax.ppermute(lax.slice_in_dim(block, block.shape[dim] - width, None, axis...]
    dot_general x17 -> x0, matrix products: 13.5 us -> none  [the longest x1 2.26 us: shards(): grad_out = jnp.dot(hidden.T, upstream, preferred_element_type=jnp.float32)]
    unnamed x41 -> x0, local copies, waits for them, and re-layouts: 11.1 us -> none
  transfers between devices with their start and end apart: 8 -> 0, of which waited for: 4 -> 0; matrix products, arithmetic and copies ran while one was open for 12% -> 0% of each run, Pallas kernels for 0% -> 0%
where the time goes in v1:
time: 44.3 us; the launch traced here: 44.1 us
  Pallas kernels  43.5 us (98%)
  between operations  0.64 us (1%)
    pallas_call x1, Pallas kernels, shards(): pl.pallas_call(kernel, out_shape=[jax.ShapeDtypeStruct(shape, dtype) for...  41.1 us
    pallas_call x1, Pallas kernels, shards(): pl.pallas_call(finish, out_shape=[jax.ShapeDtypeStruct(shape, F32) for sh...  2.37 us

profile of v1, /device:TPU:1, one launch (start us, length us, event | category | flops | bytes accessed | tf_op | source)
XLA Modules:
  0.0 44.1 jit_solution(6787561889050588564)
XLA Ops:
  0.6 41.1 %edge_update.1 = (bf16[7,16,128]{2,1,0:T(8,128)(2,1)}, bf16[7,32,128]{2,1,0:T(8,128)(2,1)}, bf16[7,16,128]{2,1,0:T(8,128)(2,1)}, f32[4,16,128]{2,1,0:T(8,128)}, f32[64,256]{1,0:T(8,128)}, /*index=5*/f32[8,8,128]{2,1,0:T(8,128)}) custom-call(bf16[256,512]{1,0:T(8,128)(2,1)} %lat_h.1, bf16[256,512]{1,0:T(8,128)(2,1)} %cot_h.1, bf16[512,256]{1,0:T(8,128)(2,1)} %ws_h.1, ...), custom_call_target="tpu_custom_call" | custom-call | tf_op jit(solution)/shard_map/edge_update/pallas_call | solution.py:506
  41.8 2.4 %finish.1 = (f32[64,256]{1,0:T(8,128)}, f32[8,256]{1,0:T(8,128)}, f32[8,256]{1,0:T(8,128)}, f32[8,256]{1,0:T(8,128)}, f32[4]{0:T(128)}) custom-call(bf16[7,16,128]{2,1,0:T(8,128)(2,1)} %get-tuple-element.16.rz0_h, bf16[7,32,128]{2,1,0:T(8,128)(2,1)} %get-tuple-element.17.rz1_h, bf16[7,16,128]{2,1,0:T(8,128)(2,1)} %get-tuple-element.18.rz2_h, ...), custom_call_target="tpu_custom_call" | custom-call | tf_op jit(solution)/shard_map/finish/pallas_call | solution.py:518

commit v2 on v1

--- a/solution.py
+++ b/solution.py
@@ -48,7 +48,7 @@
     lat_h, cot_h, ws_h, wr_h, bias_h, wo_h, fs_h, fr_h, fv_h, sr_h, cs_h, cr_h, cv_h,
     rz0, rz1, rz2, own_h, node_h, rcy,
     low, lat, cot, ws, wr, bias, wo, fs, fr, fv, sr, cs, cr, cv, load_sem,
-    msg32, zrow, zrow32, zraw, zraw32, pick_s, pick_t, psel, prow, praw_s, praw_r, halo, wst, latt, cott, a_src, a_rcv, a_slot,
+    msg32, zrow, zrow32, zraw, zraw32, pick_s, pick_t, psel, prow, praw_s, praw_r, halo, wst, latt, cott, a_src, a_rcv, a_slot, oh_s, oh_r, oh_c, pre_in, back_in,
     g_src, g_rh, g_slot,
     ret_s, ret_r, col_s, col_r, rim_s, rim_r,
     buf0, buf1, buf2, rc0, rc1, rc2, xs0, xs1, xs2, rx0, rx1, rx2, sums, own, zs0, zs1, zs2,
@@ -160,11 +160,35 @@
     a_rcv[H : 2 * H, :] = lo
     a_rcv[2 * H : 3 * H, :] = nt(wo[...], cot[...]).astype(BF)
 
+    for k in range(4):
+        at = slice(k * CH, (k + 1) * CH)
+        ends, live = (fr[at], fv[at]) if k < 3 else (cr[0, :], cv[0, :])
+        oh_r[k] = one_hot(ROWS, ends.reshape(1, CH))
+        from_r = nn(a_rcv[...], oh_r[k])
+        back_in[k] = from_r[2 * H :] * live.reshape(1, CH).astype(F32)
+        pre = from_r[0:H] + from_r[H : 2 * H]
+        if k < 3:
+            s = fs[at].reshape(1, CH)
+            s = jnp.where(s < HALO, s + ROWS, jnp.where(s < HALO + ROWS, s - HALO, s))
+            oh_s[k] = one_hot(ROWS + 2 * HALO, s)
+            from_s = nn(a_src[:, 0:ROWS], oh_s[k, 0:ROWS, :])
+            pre += from_s[0:H] + from_s[H : 2 * H]
+        pre_in[k] = pre
+
     wide = lax.broadcasted_iota(jnp.int32, (256, 128), 0)
     lane = lax.broadcasted_iota(jnp.int32, (256, 128), 1)
     spread = (lane == (wide & 7) * 16 + ((wide >> 3) & 3)).astype(F32).astype(BF)
     asked = ((z * XS + ((x + (wide >> 6)) & (XS - 1))) << 1) + ((c + (wide >> 5)) & 1)
     here = lane == asked
+    q = cs[...]
+    place = (
+        (((x + XS - ((q >> 3) & (XS - 1))) & (XS - 1)) << 6)
+        + (((c + (q >> 2)) & 1) << 5)
+        + ((q & 3) << 3)
+        + ((z + ZS - (q >> 5)) & (ZS - 1))
+    )
+    oh_c[...] = one_hot(256, place)
+
     for copy in z_rows:
         copy.wait()
     zrow32[...] = zrow[...].astype(F32)
@@ -181,6 +205,18 @@
     for copy in p_rows:
         copy.start()
     prow[0] = psel[0]
+    for copy in z_raws:
+        copy.wait()
+    zraw32[...] = zraw[...].astype(F32)
+    for i in range(4):
+        rows = zraw32[:, 8 * i : 8 * i + 8, :].reshape(64, 128).astype(BF)
+        praw_s[:, :, 128 * i : 128 * i + 128] = nn(pick_s[...], rows).astype(BF).reshape(8, 32, 128)
+    p_raws = [
+        remote(praw_s.at[m], praw_r.at[m], pr_sem, m - 1, nodes=plane(m, 1)) for m in (4, 5, 2, 3, 6, 7, 1)
+    ]
+    for copy in p_raws:
+        copy.start()
+    praw_r[0] = praw_s[0]
     pick_t[...] = nt(eye(64), pick_s[...]).astype(BF)
 
     for copy in halos:
@@ -194,47 +230,24 @@
     a_src[0:H, ROWS : ROWS + 2 * HALO] = hi
     a_src[H : 2 * H, ROWS : ROWS + 2 * HALO] = lo
 
-    def edges(source, send_row, recv_row, live_row, count, exact):
-        pick_s = one_hot(count, send_row)
-        pick_r = one_hot(ROWS, recv_row)
-        from_s = nn(source[...], pick_s)
-        from_r = nn(a_rcv[...], pick_r)
-        live = live_row.astype(F32)
-        pre = from_s[0:H] + from_r[0:H] + from_r[H : 2 * H]
-        if exact:
-            pre += from_s[H : 2 * H]
+    def edges(k, from_s, live_row):
+        pre = pre_in[k] + from_s
         sig = 0.5 + 0.5 * jnp.tanh(0.5 * pre)
         act = pre * sig
         slope = sig + act * (1.0 - sig)
-        grad = (from_r[2 * H :] * live * slope).astype(BF)
-        hidden = (act * live).astype(BF)
-        return pick_s, pick_r, grad, hidden
+        return (back_in[k] * slope).astype(BF), (act * live_row.astype(F32)).astype(BF)
 
     for k in range(FINE // CH):
         at = slice(k * CH, (k + 1) * CH)
-        s = fs[at].reshape(1, CH)
-        s = jnp.where(s < HALO, s + ROWS, jnp.where(s < HALO + ROWS, s - HALO, s))
-        by_s, by_r, grad, hidden = edges(a_src, s, fr[at].reshape(1, CH), fv[at].reshape(1, CH), ROWS + 2 * HALO, True)
-        add_s, add_r = nt(by_s, grad), nt(by_r, jnp.concatenate([grad, hidden], 0))
+        from_s = nn(a_src[:, ROWS : ROWS + 2 * HALO], oh_s[k, ROWS : ROWS + 2 * HALO, :])
+        grad, hidden = edges(k, from_s[0:H] + from_s[H : 2 * H], fv[at].reshape(1, CH))
+        add_s, add_r = nt(oh_s[k], grad), nt(oh_r[k], jnp.concatenate([grad, hidden], 0))
         if k == 0:
             g_src[...] = add_s
             g_rh[...] = add_r
         else:
             g_src[...] += add_s
             g_rh[...] += add_r
-        if k == 0:
-            for copy in z_raws:
-                copy.wait()
-            zraw32[...] = zraw[...].astype(F32)
-            for i in range(4):
-                rows = zraw32[:, 8 * i : 8 * i + 8, :].reshape(64, 128).astype(BF)
-                praw_s[:, :, 128 * i : 128 * i + 128] = nn(pick_s[...], rows).astype(BF).reshape(8, 32, 128)
-            p_raws = [
-                remote(praw_s.at[m], praw_r.at[m], pr_sem, m - 1, nodes=plane(m, 1)) for m in (4, 5, 2, 3, 6, 7, 1)
-            ]
-            for copy in p_raws:
-                copy.start()
-            praw_r[0] = praw_s[0]
 
     rim_s[...] = g_src[ROWS : ROWS + 2 * HALO, :].astype(BF)
     rims = (
@@ -247,14 +260,7 @@
     for copy in p_rows:
         copy.wait()
     a_slot[...] = nt(eye256, prow[...].reshape(256, H)).astype(BF)
-    q = cs[...]
-    place = (
-        (((x + XS - ((q >> 3) & (XS - 1))) & (XS - 1)) << 6)
-        + (((c + (q >> 2)) & 1) << 5)
-        + ((q & 3) << 3)
-        + ((z + ZS - (q >> 5)) & (ZS - 1))
-    )
-    by_s, by_r, grad, hidden = edges(a_slot, place, cr[...], cv[...], 256, False)
+    grad, hidden = edges(3, nn(a_slot[...], oh_c[...]), cv[...])
 
     bufs, rcs, xss, rxs = (buf0, buf1, buf2), (rc0, rc1, rc2), (xs0, xs1, xs2), (rx0, rx1, rx2)
     zss, rzs = (zs0, zs1, zs2), (rz0, rz1, rz2)
@@ -285,17 +291,17 @@
             copy.start()
             x_copies.append(copy)
 
-    lay_out(buf0, nn(cott[...], (g_rh[:, H : 2 * H] + nt(by_r, hidden)).astype(BF)))
-    send_core(0)
-
-    g_slot[...] = nt(by_s, grad).astype(BF)
+    g_slot[...] = nt(oh_c[...], grad).astype(BF)
     ret_s[...] = g_slot[...].reshape(8, 32, H)
     backs = [remote(ret_s.at[m], ret_r.at[m], rp_sem, m - 1, nodes=plane(m, -1)) for m in (4, 5, 2, 3, 6, 7, 1)]
     for copy in backs:
         copy.start()
     ret_r[0] = ret_s[0]
 
-    g_recv = g_rh[:, 0:H] + nt(by_r, grad)
+    lay_out(buf0, nn(cott[...], (g_rh[:, H : 2 * H] + nt(oh_r[3], hidden)).astype(BF)))
+    send_core(0)
+
+    g_recv = g_rh[:, 0:H] + nt(oh_r[3], grad)
     lay_out(buf1, nn(latt[:, 0:ROWS], g_recv.astype(BF)))
     total = jnp.sum(g_recv, axis=0, keepdims=True)
     bias_tile = jnp.concatenate([total[:, 0:128], total[:, 128:256], jnp.zeros((14, 128), F32)], 0).astype(BF)
@@ -318,11 +324,13 @@
 
     for copy in rims:
         copy.wait()
+    low_rows = g_src[0:HALO, :]
     low = jnp.where(b == 0, 0.0, rim_r[0:HALO, :].astype(F32))
     high = jnp.where(b == NODES - 1, 0.0, rim_r[HALO : 2 * HALO, :].astype(F32))
-    g_src[0:HALO, :] += low
-    g_src[ROWS - HALO : ROWS, :] += high
-    node = nt(ws[...], g_src[0:ROWS, :].astype(BF)) + nt(wr[...], g_recv.astype(BF))
+    sent = jnp.concatenate(
+        [low_rows + low, g_src[HALO : ROWS - HALO, :], g_src[ROWS - HALO : ROWS, :] + high], 0
+    )
+    node = nt(ws[...], sent.astype(BF)) + nt(wr[...], g_recv.astype(BF))
     part[...] = node.reshape(HID, 64, ROWS)
     ys[...] = node.astype(BF).reshape(HID, 64, ROWS)
     y_copies = []
@@ -336,7 +344,9 @@
 
     for copy in backs:
         copy.wait()
-    col_s[...] = nn(pick_t[...], ret_r[...].reshape(256, H)).reshape(ZS, 8, H)
+    summed = nn(pick_t[...], ret_r[...].reshape(256, H)).reshape(ZS, 8, H)
+    for k in range(ZS):
+        col_s[k] = jnp.concatenate([summed[k, :, 0:128], summed[k, :, 128:256]], 0).astype(BF)
     cols = [remote(col_s.at[k], col_r.at[k], rz_sem, k - 1, nodes=column(k, -1)) for k in (4, 3, 5, 2, 6, 1, 7)]
     for copy in cols:
         copy.start()
@@ -369,9 +379,10 @@
 
     for copy in cols:
         copy.wait()
-    coarse = col_r[0]
+    tile = col_r[0].astype(F32)
     for k in range(1, ZS):
-        coarse += col_r[k]
+        tile += col_r[k].astype(F32)
+    coarse = jnp.concatenate([tile[0:8], tile[8:16]], 1)
     coarse = jnp.concatenate([coarse, jnp.zeros((8, H), F32)], 0)
     hi, lo = split(coarse)
     coarse_part = nt(hi, ws[...]) + nt(lo, ws[...])
@@ -403,7 +414,7 @@
 def finish(
     rz0_h, rz1_h, rz2_h, own_h, node_h, rcy_h,
     n_out, s_out, r_out, o_out, b_out,
-    rz0, rz1, rz2, own, node, rcy, n_v, s_v, r_v, o_v, in_sem, out_sem,
+    rz0, rz1, rz2, own, node, rcy, n_v, s_v, r_v, o_v, b_v, in_sem, out_sem,
 ):
     b = lax.axis_index("nodes")
     y = lax.axis_index("hid")
@@ -441,7 +452,8 @@
     rest = line - v0.astype(F32)
     v1 = rest.astype(BF)
     v2 = (rest - v1.astype(F32)).astype(BF)
-    b_out[...] = (nn(v0, take) + nn(v1, take) + nn(v2, take))[0, 0:4]
+    b_v[...] = (nn(v0, take) + nn(v1, take) + nn(v2, take))[0, 0:4]
+    write(4, b_v, b_out)
 
     reads[4].wait()
     late = rcy[HID - 1]
@@ -480,8 +492,9 @@
         vm((8, 32, H), BF), vm((8, 32, H), BF), vm((8, 32, D), BF), vm((8, 32, D), BF),
         vm((2 * HALO, D), BF), vm((H, D), BF), vm((D, 640), BF), vm((D, ROWS), BF),
         vm((2 * H, 384), BF), vm((3 * H, ROWS), BF), vm((H, 256), BF),
+        vm((3, 384, CH), BF), vm((4, ROWS, CH), BF), vm((256, CH), BF), vm((4, H, CH), F32), vm((4, H, CH), F32),
         vm((384, H), F32), vm((ROWS, 2 * H), F32), vm((256, H), BF),
-        vm((8, 32, H), BF), vm((8, 32, H), BF), vm((ZS, 8, H), F32), vm((ZS, 8, H), F32),
+        vm((8, 32, H), BF), vm((8, 32, H), BF), vm((ZS, 16, 128), BF), vm((ZS, 16, 128), BF),
         vm((2 * HALO, H), BF), vm((2 * HALO, H), BF),
     ]
     scratch += [vm((2, XS, t, 16, 128), BF) for t in TILES]
@@ -519,10 +532,10 @@
         finish,
         out_shape=[jax.ShapeDtypeStruct(shape, F32) for shape in results + [(4,)]],
         in_specs=[hbm] * 6,
-        out_specs=[hbm] * 4 + [pl.BlockSpec(memory_space=pltpu.VMEM)],
+        out_specs=[hbm] * 5,
         scratch_shapes=[vm(shape, dtype) for shape, dtype in kept]
-        + [vm(shape, F32) for shape in results]
-        + [sems((6,)), sems((4,))],
+        + [vm(shape, F32) for shape in results + [(4,)]]
+        + [sems((6,)), sems((5,))],
         compiler_params=pltpu.CompilerParams(vmem_limit_bytes=64 * 1024 * 1024),
         name="finish",
     )(*arrived)

time: 44.3 us -> 42.5 us (0.959)
  Pallas kernels: 43.5 us -> 41.6 us
    pallas_call x1, Pallas kernels: 41.1 us -> 39.8 us  [shards(): pl.pallas_call(kernel, out_shape=[jax.ShapeDtypeStruct(shape, dtype) for...]
    pallas_call x1, Pallas kernels: 2.37 us -> 1.87 us  [shards(): pl.pallas_call(finish, out_shape=[jax.ShapeDtypeStruct(shape, F32) for sh...]
where the time goes in v2:
time: 42.5 us; the launch traced here: 42.3 us
  Pallas kernels  41.6 us (98%)
  between operations  0.64 us (2%)
    pallas_call x1, Pallas kernels, shards(): pl.pallas_call(kernel, out_shape=[jax.ShapeDtypeStruct(shape, dtype) for...  39.8 us
    pallas_call x1, Pallas kernels, shards(): pl.pallas_call(finish, out_shape=[jax.ShapeDtypeStruct(shape, F32) for sh...  1.87 us

profile of v2, /device:TPU:1, one launch (start us, length us, event | category | flops | bytes accessed | tf_op | source)
XLA Modules:
  0.0 42.3 jit_solution(14851470568937561845)
XLA Ops:
  0.6 39.8 %edge_update.1 = (bf16[7,16,128]{2,1,0:T(8,128)(2,1)}, bf16[7,32,128]{2,1,0:T(8,128)(2,1)}, bf16[7,16,128]{2,1,0:T(8,128)(2,1)}, f32[4,16,128]{2,1,0:T(8,128)}, f32[64,256]{1,0:T(8,128)}, /*index=5*/f32[8,8,128]{2,1,0:T(8,128)}) custom-call(bf16[256,512]{1,0:T(8,128)(2,1)} %lat_h.1, bf16[256,512]{1,0:T(8,128)(2,1)} %cot_h.1, bf16[512,256]{1,0:T(8,128)(2,1)} %ws_h.1, ...), custom_call_target="tpu_custom_call" | custom-call | tf_op jit(solution)/shard_map/edge_update/pallas_call | solution.py:519
  40.4 1.9 %finish.1 = (f32[64,256]{1,0:T(8,128)}, f32[8,256]{1,0:T(8,128)}, f32[8,256]{1,0:T(8,128)}, f32[8,256]{1,0:T(8,128)}, f32[4]{0:T(128)}) custom-call(bf16[7,16,128]{2,1,0:T(8,128)(2,1)} %get-tuple-element.16.rz0_h, bf16[7,32,128]{2,1,0:T(8,128)(2,1)} %get-tuple-element.17.rz1_h, bf16[7,16,128]{2,1,0:T(8,128)(2,1)} %get-tuple-element.18.rz2_h, ...), custom_call_target="tpu_custom_call" | custom-call | tf_op jit(solution)/shard_map/finish/pallas_call | solution.py:531

commit v3 on v2

--- a/solution.py
+++ b/solution.py
@@ -88,13 +88,15 @@
     def greet(**device):
         pl.semaphore_signal(bar, inc=1, device_id=device, device_id_type=MESH)
 
-    for k in (4, 3, 5, 2, 6, 1, 7):
+    for k in (4, 3, 5):
         greet(nodes=column(k, 1))
-    for m in (4, 5, 2, 3, 6, 7, 1):
+        greet(hid=lax.rem(y + k, HID))
+    for m in (5, 4, 3, 2, 7, 6, 1):
         greet(nodes=plane(m, 1))
+    for k in (2, 6, 1, 7):
+        greet(nodes=column(k, 1))
+        greet(hid=lax.rem(y + k, HID))
     greet(nodes=lax.rem(b + NODES - 1 + 2 * c, NODES))
-    for k in (4, 3, 5, 2, 6, 1, 7):
-        greet(hid=lax.rem(y + k, HID))
     for load in loads[2:]:
         load.start()
 
@@ -123,6 +125,9 @@
     z_rows = [remote(zrow.at[0], zrow.at[k], zg_sem, k - 1, nodes=column(k, 1)) for k in (4, 3, 5, 2, 6, 1, 7)]
     for copy in z_rows:
         copy.start()
+    z_raws = [remote(zraw.at[0], zraw.at[k], zr_sem, k - 1, nodes=column(k, 1)) for k in (4, 3, 5, 2, 6, 1, 7)]
+    for copy in z_raws:
+        copy.start()
     loads[2].wait()
     up = lax.rem(b + 1, NODES)
     down = lax.rem(b + NODES - 1, NODES)
@@ -133,9 +138,6 @@
     for copy in halos:
         copy.start()
 
-    z_raws = [remote(zraw.at[0], zraw.at[k], zr_sem, k - 1, nodes=column(k, 1)) for k in (4, 3, 5, 2, 6, 1, 7)]
-    for copy in z_raws:
-        copy.start()
 
     for load in loads[3:]:
         load.wait()
@@ -201,7 +203,7 @@
     for k in range(2):
         rows = zrow32[:, 8 * k : 8 * k + 8, :].reshape(64, 128).astype(BF)
         psel[:, :, 128 * k : 128 * k + 128] = nn(pick_s[...], rows).astype(BF).reshape(8, 32, 128)
-    p_rows = [remote(psel.at[m], prow.at[m], pg_sem, m - 1, nodes=plane(m, 1)) for m in (4, 5, 2, 3, 6, 7, 1)]
+    p_rows = [remote(psel.at[m], prow.at[m], pg_sem, m - 1, nodes=plane(m, 1)) for m in (5, 4, 3, 2, 7, 6, 1)]
     for copy in p_rows:
         copy.start()
     prow[0] = psel[0]
@@ -212,7 +214,7 @@
         rows = zraw32[:, 8 * i : 8 * i + 8, :].reshape(64, 128).astype(BF)
         praw_s[:, :, 128 * i : 128 * i + 128] = nn(pick_s[...], rows).astype(BF).reshape(8, 32, 128)
     p_raws = [
-        remote(praw_s.at[m], praw_r.at[m], pr_sem, m - 1, nodes=plane(m, 1)) for m in (4, 5, 2, 3, 6, 7, 1)
+        remote(praw_s.at[m], praw_r.at[m], pr_sem, m - 1, nodes=plane(m, 1)) for m in (5, 4, 3, 2, 7, 6, 1)
     ]
     for copy in p_raws:
         copy.start()
@@ -230,12 +232,12 @@
     a_src[0:H, ROWS : ROWS + 2 * HALO] = hi
     a_src[H : 2 * H, ROWS : ROWS + 2 * HALO] = lo
 
-    def edges(k, from_s, live_row):
-        pre = pre_in[k] + from_s
+    def edges(k, from_s, live_row, at=slice(0, CH)):
+        pre = pre_in[k, :, at] + from_s
         sig = 0.5 + 0.5 * jnp.tanh(0.5 * pre)
         act = pre * sig
         slope = sig + act * (1.0 - sig)
-        return (back_in[k] * slope).astype(BF), (act * live_row.astype(F32)).astype(BF)
+        return (back_in[k, :, at] * slope).astype(BF), (act * live_row.astype(F32)).astype(BF)
 
     for k in range(FINE // CH):
         at = slice(k * CH, (k + 1) * CH)
@@ -260,7 +262,12 @@
     for copy in p_rows:
         copy.wait()
     a_slot[...] = nt(eye256, prow[...].reshape(256, H)).astype(BF)
-    grad, hidden = edges(3, nn(a_slot[...], oh_c[...]), cv[...])
+    halves = []
+    for k in range(2):
+        at = slice(k * CH // 2, (k + 1) * CH // 2)
+        halves.append(edges(3, nn(a_slot[...], oh_c[:, at]), cv[:, at], at))
+    grad = jnp.concatenate([half[0] for half in halves], 1)
+    hidden = jnp.concatenate([half[1] for half in halves], 1)
 
     bufs, rcs, xss, rxs = (buf0, buf1, buf2), (rc0, rc1, rc2), (xs0, xs1, xs2), (rx0, rx1, rx2)
     zss, rzs = (zs0, zs1, zs2), (rz0, rz1, rz2)
@@ -282,9 +289,9 @@
 
     def send_x(a):
         cores[a].wait()
-        xss[a][...] = (bufs[a][c].astype(F32) + rcs[a][...].astype(F32)).astype(BF)
         for k in (2, 1, 3):
             to = lax.rem(x + k, XS)
+            xss[a][to] = (bufs[a][c, to].astype(F32) + rcs[a][to].astype(F32)).astype(BF)
             copy = remote(
                 xss[a].at[to], rxs[a].at[k - 1], x_sem, 3 * a + k - 1, nodes=(z * XS + to) * 2 + c
             )
@@ -293,7 +300,7 @@
 
     g_slot[...] = nt(oh_c[...], grad).astype(BF)
     ret_s[...] = g_slot[...].reshape(8, 32, H)
-    backs = [remote(ret_s.at[m], ret_r.at[m], rp_sem, m - 1, nodes=plane(m, -1)) for m in (4, 5, 2, 3, 6, 7, 1)]
+    backs = [remote(ret_s.at[m], ret_r.at[m], rp_sem, m - 1, nodes=plane(m, -1)) for m in (5, 4, 3, 2, 7, 6, 1)]
     for copy in backs:
         copy.start()
     ret_r[0] = ret_s[0]

time: 42.5 us -> 42.6 us (level)
  no operation moved by 1% of the time
where the time goes in v3:
time: 42.6 us; the launch traced here: 42.4 us
  Pallas kernels  41.7 us (98%)
  between operations  0.64 us (2%)
    pallas_call x1, Pallas kernels, shards(): pl.pallas_call(kernel, out_shape=[jax.ShapeDtypeStruct(shape, dtype) for...  39.9 us
    pallas_call x1, Pallas kernels, shards(): pl.pallas_call(finish, out_shape=[jax.ShapeDtypeStruct(shape, F32) for sh...  1.87 us

profile of v3, /device:TPU:1, one launch (start us, length us, event | category | flops | bytes accessed | tf_op | source)
XLA Modules:
  0.0 42.4 jit_solution(16434633597063756186)
XLA Ops:
  0.6 39.9 %edge_update.1 = (bf16[7,16,128]{2,1,0:T(8,128)(2,1)}, bf16[7,32,128]{2,1,0:T(8,128)(2,1)}, bf16[7,16,128]{2,1,0:T(8,128)(2,1)}, f32[4,16,128]{2,1,0:T(8,128)}, f32[64,256]{1,0:T(8,128)}, /*index=5*/f32[8,8,128]{2,1,0:T(8,128)}) custom-call(bf16[256,512]{1,0:T(8,128)(2,1)} %lat_h.1, bf16[256,512]{1,0:T(8,128)(2,1)} %cot_h.1, bf16[512,256]{1,0:T(8,128)(2,1)} %ws_h.1, ...), custom_call_target="tpu_custom_call" | custom-call | tf_op jit(solution)/shard_map/edge_update/pallas_call | solution.py:526
  40.5 1.9 %finish.1 = (f32[64,256]{1,0:T(8,128)}, f32[8,256]{1,0:T(8,128)}, f32[8,256]{1,0:T(8,128)}, f32[8,256]{1,0:T(8,128)}, f32[4]{0:T(128)}) custom-call(bf16[7,16,128]{2,1,0:T(8,128)(2,1)} %get-tuple-element.16.rz0_h, bf16[7,32,128]{2,1,0:T(8,128)(2,1)} %get-tuple-element.17.rz1_h, bf16[7,16,128]{2,1,0:T(8,128)(2,1)} %get-tuple-element.18.rz2_h, ...), custom_call_target="tpu_custom_call" | custom-call | tf_op jit(solution)/shard_map/finish/pallas_call | solution.py:538
